TPU v7x, 512 devices: a whole 4x8x8 slice. The times are simulated.
512 devices in a mesh: ctx: 64 (over y, x, core), head: 8 (over z).
Axes of the slice: x: 4, y: 8, z: 8, core: 2. Of those that a mesh axis runs over, the one named last changes fastest.
Arguments:
- queries: bfloat16 [16384, 2048], P('ctx', 'head'), may hold values from -160 to 160
- keys: bfloat16 [16384, 2048], P('ctx', 'head'), may hold values from -6 to 6
- values: bfloat16 [16384, 2048], P('ctx', 'head'), may hold values from -6 to 6
- group_lens: int32 [32], replicated, may hold values from 1 to 1024, 16384 in all
- dispatch: int32 [256], replicated, may hold values from 0 to 255, each once
- out_weight: bfloat16 [2048, 3072], P('head'), may hold values from -0.125 to 0.125
Outputs:
- mixed: bfloat16 [16384, 3072], P(('ctx', 'head'))
Inputs may be any that keep to these rules, and one draw needn't show every extreme that they name: `dispatch`: each slice number appears once. `group_lens`: positive, summing to 16384, the largest exactly 1024.
All inputs are finite; a program needn't handle non-finite values.
Results may differ from a plain program's by a relative error of at most 0.02.
Values may be sent and summed in bfloat16 or wider, within the bound.
A program may use at most 128 MiB of HBM per device.

v0:
```python
import math

import jax
import jax.numpy as jnp
from jax import lax
from jax.sharding import PartitionSpec as P

HEAD_DIM = 128
SLICE = 64


def group_numbers(dispatch, group_ends, first_row, row_count):
    slot_start = first_row // SLICE
    slot_numbers = lax.dynamic_slice_in_dim(dispatch, slot_start, row_count // SLICE)
    positions = (
        slot_numbers[:, None] * SLICE + jnp.arange(SLICE, dtype=jnp.int32)[None, :]
    ).reshape(row_count)
    return jnp.sum((group_ends[None, :] <= positions[:, None]).astype(jnp.int32), axis=1)


def update(carried, query_rows, query_marks, key_block, value_block, group_block, scale):
    running_max, running_sum, weighted = carried
    scores = (
        jnp.einsum("qhd,khd->hqk", query_rows, key_block, preferred_element_type=jnp.float32)
        * scale
    )
    allowed = (group_block[None, :] <= query_marks[:, None])[None]
    masked = jnp.where(allowed, scores, -1e30)
    new_max = jnp.maximum(running_max, jnp.max(masked, axis=2))
    weights = jnp.where(allowed, jnp.exp(scores - new_max[..., None]), 0.0)
    factor = jnp.exp(running_max - new_max)
    new_sum = running_sum * factor + jnp.sum(weights, axis=2)
    summed = jnp.einsum(
        "hqk,khd->hqd",
        weights.astype(jnp.bfloat16),
        value_block,
        preferred_element_type=jnp.float32,
    )
    return (new_max, new_sum, weighted * factor[..., None] + summed)


def body(queries, keys, values, group_lens, dispatch, out_weight):
    row_count = queries.shape[0]
    feature_width = queries.shape[1]
    local_heads = feature_width // HEAD_DIM
    scale = HEAD_DIM ** (-0.5)
    group_ends = jnp.cumsum(group_lens)
    first_row = lax.axis_index("ctx") * row_count
    query_groups = group_numbers(dispatch, group_ends, first_row, row_count)
    query_heads = queries.reshape(row_count, local_heads, HEAD_DIM)
    initial = (
        jnp.full((local_heads, row_count), -1e30, jnp.float32),
        jnp.zeros((local_heads, row_count), jnp.float32),
        jnp.zeros((local_heads, row_count, HEAD_DIM), jnp.float32),
    )
    key_part = lax.all_gather(keys, "ctx", axis=0, tiled=True)
    value_part = lax.all_gather(values, "ctx", axis=0, tiled=True)
    piece_rows = key_part.shape[0]
    key_groups = group_numbers(dispatch, group_ends, jnp.int32(0), piece_rows)
    block_rows = math.gcd(piece_rows, 512)
    block_count = piece_rows // block_rows
    key_blocks = key_part.reshape(block_count, block_rows, local_heads, HEAD_DIM)
    value_blocks = value_part.reshape(block_count, block_rows, local_heads, HEAD_DIM)
    group_blocks = key_groups.reshape(block_count, block_rows)

    def advance(state, block_triple):
        key_block, value_block, group_block = block_triple
        return (
            update(state, query_heads, query_groups, key_block, value_block, group_block, scale),
            None,
        )

    result, unused = lax.scan(advance, initial, (key_blocks, value_blocks, group_blocks))
    running_max, running_sum, weighted = result
    attended = (
        (weighted / running_sum[..., None])
        .transpose(1, 0, 2)
        .reshape(row_count, feature_width)
        .astype(jnp.bfloat16)
    )
    return lax.psum_scatter(
        jnp.dot(attended, out_weight, preferred_element_type=jnp.float32).astype(jnp.bfloat16),
        "head",
        scatter_dimension=0,
        tiled=True,
    )


def solution(mesh):
    return jax.shard_map(
        body,
        mesh=mesh,
        in_specs=(P("ctx", "head"), P("ctx", "head"), P("ctx", "head"), P(), P(), P("head", None)),
        out_specs=P(("ctx", "head"), None),
        check_vma=False,
    )
```

profile of v0, /device:TPU:1, one launch (start us, length us, event | category | flops | bytes accessed | tf_op | source)
XLA Modules:
  0.0 338.9 jit_solution(2692143877132939700)
XLA Ops:
  12.5 92.3 %all-gather.3.cloned.1.call-done = bf16[16384,256]{1,0:T(8,128)(2,1)} async-done(((bf16[256,256]{1,0:T(8,128)(2,1)}), bf16[16384,256]{1,0:T(8,128)(2,1)}) %all-gather.3.cloned.1.call-update) | async-done | bytes 8388624 | tf_op jit(solution)/shard_map/all_gather | solution.py:56
  104.8 12.5 %reshape.107 = bf16[32,512,2,128]{3,2,1,0:T(2,128)(2,1)} reshape(bf16[16384,256]{1,0:T(8,128)(2,1)} %all-gather.3.cloned.1.call-done) | data formatting | bytes 16777216 | tf_op jit(solution)/shard_map/reshape | solution.py:62
  117.3 76.6 %all-gather.5.cloned.1.call-done = bf16[16384,256]{1,0:T(8,128)(2,1)} async-done(((bf16[256,256]{1,0:T(8,128)(2,1)}), bf16[16384,256]{1,0:T(8,128)(2,1)}) %all-gather.5.cloned.1.call-update) | async-done | bytes 8388624 | tf_op jit(solution)/shard_map/all_gather | solution.py:57
  193.9 12.5 %reshape.108 = bf16[32,512,2,128]{3,2,1,0:T(2,128)(2,1)} reshape(bf16[16384,256]{1,0:T(8,128)(2,1)} %all-gather.5.cloned.1.call-done) | data formatting | bytes 16777216 | tf_op jit(solution)/shard_map/reshape | solution.py:63
  206.5 86.7 %while.15 = (s32[]{:T(128)}, f32[2,256]{1,0:T(2,128)S(1)}, f32[2,256]{1,0:T(2,128)S(1)}, f32[2,256,128]{2,1,0:T(8,128)S(1)}, s32[32,512]{1,0:T(8,128)S(1)}, /*in...) while((s32[]{:T(128)}, f32[2,256]{1,0:T(2,128)S(1)}, ...), condition=%wide.region_6.7_spmd.clone, body=%wide.region_3.6_spmd.clone.sunk | while | flops 136907264 | bytes 5938313 | solution.py:73
  206.6 1.4 constant_dynamic-slice_fusion.6
  209.3 1.4 constant_dynamic-slice_fusion.6
  212.0 1.4 constant_dynamic-slice_fusion.6
  214.7 1.4 constant_dynamic-slice_fusion.6
  217.5 1.4 constant_dynamic-slice_fusion.6
  220.2 1.4 constant_dynamic-slice_fusion.6
  222.9 1.4 constant_dynamic-slice_fusion.6
  225.6 1.4 constant_dynamic-slice_fusion.6
  228.3 1.4 constant_dynamic-slice_fusion.6
  231.0 1.4 constant_dynamic-slice_fusion.6
  233.7 1.4 constant_dynamic-slice_fusion.6
  236.4 1.4 constant_dynamic-slice_fusion.6
  239.1 1.4 constant_dynamic-slice_fusion.6
  241.9 1.4 constant_dynamic-slice_fusion.6
  244.6 1.4 constant_dynamic-slice_fusion.6
  247.3 1.4 constant_dynamic-slice_fusion.6
  250.0 1.4 constant_dynamic-slice_fusion.6
  263.6 1.4 constant_dynamic-slice_fusion.6
  266.3 1.4 constant_dynamic-slice_fusion.6
  269.0 1.4 constant_dynamic-slice_fusion.6
  271.7 1.4 constant_dynamic-slice_fusion.6
  274.4 1.4 constant_dynamic-slice_fusion.6
  277.1 1.4 constant_dynamic-slice_fusion.6
  279.8 1.4 constant_dynamic-slice_fusion.6
  282.5 1.4 constant_dynamic-slice_fusion.6
  293.4 1.8 convolution_convert_fusion
  295.2 37.3 %reduce-scatter.2.cloned.1.call-done = bf16[32,3072]{1,0:T(8,128)(2,1)} async-done(((bf16[256,3072]{1,0:T(8,128)(2,1)}), bf16[32,3072]{1,0:T(8,128)(2,1)}) %reduce-scatter.2.cloned.1.call-update) | async-done | bytes 196624 | tf_op jit(solution)/shard_map/reduce_scatter | solution.py:81
  (290 shorter events, 55.8 us)
Async XLA Ops:
  6.5 286.8 %copy-start = (bf16[256,3072]{1,0:T(8,128)(2,1)S(1)}, bf16[256,3072]{1,0:T(8,128)(2,1)}, u32[]{:S(2)}) copy-start(bf16[256,3072]{1,0:T(8,128)(2,1)} %param.13) | copy-start | bytes 4718596
  6.5 98.2 %all-gather.3.cloned.1.call-start = ((), (), s32[]{:S(2)}) async-start(), calls=%async_computation.1 | async-start | bytes 8519680 | tf_op jit(solution)/shard_map/all_gather | solution.py:56
  7.3 186.7 %all-gather.5.cloned.1.call-start = ((), (), s32[]{:S(2)}) async-start(), calls=%async_computation.2 | async-start | bytes 8519680 | tf_op jit(solution)/shard_map/all_gather | solution.py:57
  8.0 324.4 %reduce-scatter.2.cloned.1.call-start = ((), (), s32[]{:S(2)}) async-start(), calls=%async_computation.3 | async-start | bytes 1769472 | tf_op jit(solution)/shard_map/reduce_scatter | solution.py:81
Sparse Core Ops, SparseCore 0:
  10.7 94.0 all-gather.2
  108.1 85.7 all-gather.4
  295.3 37.0 reduce-scatter.1
where the time goes:
time: 343 us; the launch traced here: 339 us
  waiting for transfers between devices  208 us (61%)
  local copies, waits for them, and re-layouts  72.4 us (21%)
  matrix products  28.9 us (8%)
  other arithmetic  14.8 us (4%)
  between operations  13.2 us (4%)
    all_gather x1, waiting for transfers between devices, body(): key_part = lax.all_gather(keys, 'ctx', axis=0, tiled=True)  92.3 us
    all_gather x1, waiting for transfers between devices, body(): value_part = lax.all_gather(values, 'ctx', axis=0, tiled=True)  76.6 us
    dynamic_slice x64, local copies, waits for them, and re-layouts, body(): lax.scan(advance, initial, (key_blocks, value_blocks, group_blocks))  45 us
    reduce_scatter x1, waiting for transfers between devices, body(): lax.psum_scatter(jnp.dot(attended, out_weight, preferred_element_type=jnp...  37.3 us
    dot_general x32, matrix products, update(): jnp.einsum('hqk,khd->hqd', weights.astype(jnp.bfloat16), value_block, pre...  17 us
    reshape x1, local copies, waits for them, and re-layouts, body(): key_part.reshape(block_count, block_rows, local_heads, HEAD_DIM)  12.5 us
    reshape x1, local copies, waits for them, and re-layouts, body(): value_part.reshape(block_count, block_rows, local_heads, HEAD_DIM)  12.5 us
    dot_general x32, matrix products, update(): jnp.einsum('qhd,khd->hqk', query_rows, key_block, preferred_element_type=...  10.1 us
  transfers between devices with their start and end apart: 3, of which 3 were waited for; matrix products, arithmetic and copies ran while one was open for 5% of the time, Pallas kernels for 0%

commit v1 on v0

v1 whole, which is shorter than its diff:
```python
import functools

import jax
import jax.numpy as jnp
from jax import lax
from jax.experimental import pallas as pl
from jax.experimental.pallas import tpu as pltpu
from jax.sharding import PartitionSpec as P

HD = 128
SLICE = 64
NX, NY, NZ = 4, 8, 8
ROWS = 256
PIECE = 128
KEYS = NX * 2 * ROWS
D = 3072
HIDDEN = -1e30
LOG2E = 1.4426950408889634
SCALE = HD**-0.5 * LOG2E
MESH = pl.DeviceIdType.MESH


def kernel(
    lens, disp, q_in, k_in, v_in, w_in, out,
    qbuf, qbias, kbuf, vbuf, konehot, score, part_o, part_l,
    yo_send, yl_send, yo_recv, yl_recv, att, att_send, wbuf, proj, z_send, z_recv,
    loc_sem, sib_s, sib_r, q_s, q_r, kv_s, kv_r, yo_s, yo_r, yl_s, yl_r, at_s, at_r, z_s, z_r,
):
    ctx, z = lax.axis_index("ctx"), lax.axis_index("head")
    c = lax.rem(ctx, 2)
    x = lax.rem(ctx // 2, NX)
    y = ctx // (2 * NX)

    def at(yy, xx, cc, zz):
        return ((yy * NX + xx) * 2 + cc, zz)

    def ring(i, step, size):
        return lax.rem(i + step + size, size)

    sibling = at(y, x, 1 - c, z)

    def y_dev(step):
        return at(ring(y, step, NY), x, c, z)

    def x_dev(step):
        return at(y, ring(x, step, NX), c, z)

    def z_dev(step):
        return at(y, x, c, ring(z, step, NZ))

    partners = [sibling] + [f(s) for f in (x_dev, y_dev, z_dev) for s in (-1, 1)]
    barrier = pltpu.get_barrier_semaphore()
    for dev in partners:
        pl.semaphore_signal(barrier, inc=1, device_id=dev, device_id_type=MESH)
    pl.semaphore_wait(barrier, len(partners))

    sent = []

    def send(src, dst, s, r, dev):
        copy = pltpu.make_async_remote_copy(
            src_ref=src, dst_ref=dst, send_sem=s, recv_sem=r, device_id=dev, device_id_type=MESH
        )
        copy.start()
        sent.append(copy)
        return copy

    mine = pl.ds(pl.multiple_of(c * HD, HD), HD)
    other = pl.ds(pl.multiple_of((1 - c) * HD, HD), HD)
    swaps = [
        send(q_in.at[:, p, :, other], qbuf.at[y, p, c], sib_s.at[p], sib_r.at[p], sibling)
        for p in range(2)
    ]
    swaps.append(send(k_in.at[:, other], kbuf.at[x, c], sib_s.at[2], sib_r.at[2], sibling))
    swaps.append(send(v_in.at[:, other], vbuf.at[x, c], sib_s.at[3], sib_r.at[3], sibling))
    local = [
        pltpu.make_async_copy(q_in.at[:, p, :, mine], qbuf.at[y, p, c], loc_sem.at[p])
        for p in range(2)
    ]
    local.append(pltpu.make_async_copy(k_in.at[:, mine], kbuf.at[x, c], loc_sem.at[2]))
    local.append(pltpu.make_async_copy(v_in.at[:, mine], vbuf.at[x, c], loc_sem.at[3]))
    local.append(pltpu.make_async_copy(w_in, wbuf, loc_sem.at[4]))
    for copy in local:
        copy.start()
    for copy in swaps:
        copy.wait_recv()
    for copy in local[:4]:
        copy.wait()

    left, right = 0, 1

    def q_send(slot, owner, dev, piece=None):
        ref = qbuf.at[owner] if piece is None else qbuf.at[owner, piece]
        return send(ref, ref, q_s.at[slot], q_r.at[slot], dev)

    def kv_send(slot, ref, owner, dev):
        return send(ref.at[owner], ref.at[owner], kv_s.at[slot], kv_r.at[slot], dev)

    q_hop = [q_send(0, y, y_dev(1)), q_send(1, y, y_dev(-1))]
    kv_hop = [
        kv_send(0, kbuf, x, x_dev(1)),
        kv_send(1, vbuf, x, x_dev(-1)),
        kv_send(2, vbuf, x, x_dev(1)),
        kv_send(3, kbuf, x, x_dev(-1)),
    ]

    lane = lax.broadcasted_iota(jnp.int32, (1, HD), 1)

    def bounds(g, carry):
        total, first, last = carry
        after = total + lens[g]
        return after, jnp.where(lane == g, total, first), jnp.where(lane == g, after, last)

    _, first, last = lax.fori_loop(
        0, 32, bounds,
        (jnp.int32(0), jnp.full((1, HD), -1, jnp.int32), jnp.zeros((1, HD), jnp.int32)),
    )
    sub64 = lax.broadcasted_iota(jnp.int32, (SLICE, HD), 0)
    sub16 = lax.broadcasted_iota(jnp.int32, (16, HD), 0)

    def key_marks(s, _):
        pos = disp[y * (KEYS // SLICE) + s] * SLICE + sub64
        inside = jnp.where((first <= pos) & (pos < last), 1.0, 0.0)
        konehot[pl.ds(pl.multiple_of(s * SLICE, SLICE), SLICE), :] = inside.astype(jnp.bfloat16)
        return 0

    lax.fori_loop(0, KEYS // SLICE, key_marks, 0)

    def query_marks(i, _):
        owner, half, s = i // 8, lax.rem(i // 4, 2), lax.rem(i, 4)
        start = disp[(owner * NX + x) * 8 + half * 4 + s] * SLICE
        for j in range(2):
            for p in range(2):
                pos = start + (j * 32 + p * 16) + sub16
                qbias[owner, p, half, 2 * s + j] = jnp.where(first > pos, HIDDEN, 0.0).astype(
                    jnp.bfloat16
                )
        return 0

    lax.fori_loop(0, NY * 8, query_marks, 0)

    q_hop[0].wait_recv()
    q_hop.append(q_send(2, ring(y, -1, NY), y_dev(1)))
    q_hop[1].wait_recv()
    q_hop.append(q_send(3, ring(y, 1, NY), y_dev(-1)))
    kv_hop[0].wait_recv()
    kv_hop.append(kv_send(4, kbuf, ring(x, -1, NX), x_dev(1)))
    kv_hop[1].wait_recv()
    kv_hop.append(kv_send(5, vbuf, ring(x, 1, NX), x_dev(-1)))
    q_hop[2].wait_recv()
    q_hop.append(q_send(4, ring(y, -2, NY), y_dev(1)))
    q_hop[3].wait_recv()
    q_hop.append(q_send(5, ring(y, 2, NY), y_dev(-1)))
    for i in (2, 3, 4, 5):
        kv_hop[i].wait_recv()
    q_hop[4].wait_recv()
    q_hop.append(q_send(6, ring(y, -3, NY), y_dev(1), 0))
    q_hop[5].wait_recv()
    q_hop.append(q_send(7, ring(y, 3, NY), y_dev(-1), 1))

    ones = jnp.ones((512, HD), jnp.bfloat16)

    def attend(owner, p):
        rows = 2 * PIECE
        qa = jnp.concatenate(
            [qbuf[owner, p].reshape(rows, HD), qbias[owner, p].reshape(rows, HD)], axis=1
        )
        peak = None
        for b in range(NX):
            ka = jnp.concatenate(
                [kbuf[b].reshape(512, HD), konehot[b * 512 : (b + 1) * 512, :]], axis=1
            )
            s = lax.dot_general(
                qa, ka, (((1,), (1,)), ((), ())), preferred_element_type=jnp.float32
            )
            score[:, b * 512 : (b + 1) * 512] = s
            for t in range(4):
                tile = s[:, t * HD : (t + 1) * HD]
                peak = tile if peak is None else jnp.maximum(peak, tile)
        peak = jnp.max(peak, axis=1, keepdims=True)
        total = jnp.zeros((rows, 2 * HD), jnp.float32)
        for b in range(NX):
            w = jnp.exp2((score[:, b * 512 : (b + 1) * 512] - peak) * SCALE).astype(jnp.bfloat16)
            va = jnp.concatenate([vbuf[b].reshape(512, HD), ones], axis=1)
            total = total + jnp.dot(w, va, preferred_element_type=jnp.float32)
        weight = total[:, HD:]
        part_o[owner, p] = total[:, :HD] / weight
        part_l[owner, p] = jnp.log2(weight) + peak * SCALE

    def attend_step(j):
        def one(i, _):
            p, short = i // 2, lax.rem(i, 2)
            way = (2 * p - 1) * (1 - 2 * short)
            attend(ring(y, way * (5 - j - short), NY), p)
            return 0

        lax.fori_loop(0, 4, one, 0)

    def merge(o, l, slot):
        box = yl_recv[slot]
        column = jnp.concatenate(
            [
                jnp.transpose(jnp.broadcast_to(box[4 * h : 4 * h + 1, :], (HD, HD)))
                for h in range(2)
            ],
            axis=0,
        )
        top = jnp.maximum(l, column)
        a, b = jnp.exp2(l - top), jnp.exp2(column - top)
        total = a + b
        o = (o * a + yo_recv[slot].astype(jnp.float32) * b) / total
        return o, top + jnp.log2(total)

    sub8 = lax.broadcasted_iota(jnp.int32, (8, HD), 0)

    def y_send(p, slot, o, l, dev):
        i = p * 7 + slot
        yo_send[i] = o.astype(jnp.bfloat16)
        halves = [jnp.transpose(l[h * HD : (h + 1) * HD, :])[:8, :] for h in range(2)]
        yl_send[i] = jnp.where(sub8 < 4, halves[0], halves[1])
        return (
            send(yo_send.at[i], yo_recv.at[i], yo_s.at[i], yo_r.at[i], dev),
            send(yl_send.at[i], yl_recv.at[i], yl_s.at[i], yl_r.at[i], dev),
        )

    hops = {}
    for copy in q_hop[6:]:
        copy.wait_recv()
    for j in range(1, 5):
        attend_step(j)
        for p in range(2):
            way = 2 * p - 1
            for short in range(2):
                if short and j == 4:
                    continue
                travel = -way if short else way
                owner = ring(y, travel * (5 - j - short), NY)
                o, l = part_o[owner, p], part_l[owner, p]
                slot = 4 * short + j - 1
                if j > 1:
                    for copy in hops[p, slot - 1]:
                        copy.wait_recv()
                    o, l = merge(o, l, p * 7 + slot - 1)
                hops[p, slot] = y_send(p, slot, o, l, y_dev(travel))

    swaps = []
    for p in range(2):
        o, l = part_o[y, p], part_l[y, p]
        for slot in (6, 3):
            for copy in hops[p, slot]:
                copy.wait_recv()
            o, l = merge(o, l, p * 7 + slot)
        o = o.astype(jnp.bfloat16)
        keep = jnp.where(c == 0, o[:PIECE], o[PIECE:])
        give = jnp.where(c == 0, o[PIECE:], o[:PIECE])
        att_send[p] = give
        swaps.append(send(att_send.at[p], att.at[p, c], at_s.at[p], at_r.at[p], sibling))
        att[p, c] = keep

    local[4].wait()

    def project(p):
        a = jnp.concatenate([att[p, 0], att[p, 1]], axis=1)

        def columns(n, _):
            cut = pl.ds(pl.multiple_of(n * 768, 768), 768)
            r = jnp.dot(a, wbuf[:, cut], preferred_element_type=jnp.float32)
            proj[p, :, :, cut] = r.reshape(NZ, 16, 768)
            return 0

        lax.fori_loop(0, D // 768, columns, 0)

    zhops = {}
    for j in range(1, 5):
        for p in range(2):
            if j == 1:
                swaps[p].wait_recv()
                project(p)
            way = 2 * p - 1
            for short in range(2):
                if short and j == 4:
                    continue
                travel = -way if short else way
                owner = ring(z, travel * (5 - j - short), NZ)
                r = proj[p, owner]
                slot = 4 * short + j - 1
                i = p * 7 + slot
                if j > 1:
                    zhops[p, slot - 1].wait_recv()
                    r = r + z_recv[i - 1].astype(jnp.float32)
                z_send[i] = r.astype(jnp.bfloat16)
                zhops[p, slot] = send(
                    z_send.at[i], z_recv.at[i], z_s.at[i], z_r.at[i], z_dev(travel)
                )
    for p in range(2):
        r = proj[p, z]
        for slot in (6, 3):
            zhops[p, slot].wait_recv()
            r = r + z_recv[p * 7 + slot].astype(jnp.float32)
        out[p * 16 : (p + 1) * 16, :] = r.astype(jnp.bfloat16)
    for copy in sent:
        copy.wait_send()


def body(queries, keys, values, group_lens, dispatch, out_weight):
    bf, f32 = jnp.bfloat16, jnp.float32
    dma = pltpu.SemaphoreType.DMA
    anywhere = pl.BlockSpec(memory_space=pl.ANY)
    smem = pl.BlockSpec(memory_space=pltpu.SMEM)
    return pl.pallas_call(
        kernel,
        out_shape=jax.ShapeDtypeStruct((ROWS // NZ, D), bf),
        in_specs=[smem, smem, anywhere, anywhere, anywhere, anywhere],
        out_specs=pl.BlockSpec(memory_space=pltpu.VMEM),
        scratch_shapes=[
            pltpu.VMEM((NY, 2, 2, NZ, 16, HD), bf),
            pltpu.VMEM((NY, 2, 2, NZ, 16, HD), bf),
            pltpu.VMEM((NX, 2, ROWS, HD), bf),
            pltpu.VMEM((NX, 2, ROWS, HD), bf),
            pltpu.VMEM((KEYS, HD), bf),
            pltpu.VMEM((2 * PIECE, KEYS), f32),
            pltpu.VMEM((NY, 2, 2 * PIECE, HD), f32),
            pltpu.VMEM((NY, 2, 2 * PIECE, HD), f32),
            pltpu.VMEM((14, 2 * PIECE, HD), bf),
            pltpu.VMEM((14, 8, HD), f32),
            pltpu.VMEM((14, 2 * PIECE, HD), bf),
            pltpu.VMEM((14, 8, HD), f32),
            pltpu.VMEM((2, 2, PIECE, HD), bf),
            pltpu.VMEM((2, PIECE, HD), bf),
            pltpu.VMEM((2 * HD, D), bf),
            pltpu.VMEM((2, NZ, 16, D), f32),
            pltpu.VMEM((14, 16, D), bf),
            pltpu.VMEM((14, 16, D), bf),
            dma((5,)), dma((4,)), dma((4,)), dma((8,)), dma((8,)), dma((6,)), dma((6,)),
            dma((14,)), dma((14,)), dma((14,)), dma((14,)), dma((2,)), dma((2,)),
            dma((14,)), dma((14,)),
        ],
        compiler_params=pltpu.CompilerParams(
            collective_id=0, has_side_effects=True, vmem_limit_bytes=48 * 1024 * 1024
        ),
        cost_estimate=pl.CostEstimate(
            flops=9_000_000_000, bytes_accessed=6_000_000, transcendentals=8_400_000
        ),
    )(
        group_lens,
        dispatch,
        queries.reshape(NZ, 2, 16, 2 * HD),
        keys,
        values,
        out_weight,
    )


def solution(mesh):
    return jax.shard_map(
        body,
        mesh=mesh,
        in_specs=(P("ctx", "head"), P("ctx", "head"), P("ctx", "head"), P(), P(), P("head", None)),
        out_specs=P(("ctx", "head"), None),
        check_vma=False,
    )
```

time: 343 us -> 89.5 us (0.26)
  the two profiles are of different devices: /device:TPU:1 before, /device:TPU:8 now
where the time goes in v1:
time: 89.5 us; the launch traced here: 89.3 us
  Pallas kernels  83.2 us (93%)
  local copies, waits for them, and re-layouts  6.13 us (7%)
    pallas_call x1, Pallas kernels, body(): pl.pallas_call(kernel, out_shape=jax.ShapeDtypeStruct((ROWS // NZ, D), bf...  83.2 us
    unnamed x13, local copies, waits for them, and re-layouts  6.13 us

profile of v1, /device:TPU:8, one launch (start us, length us, event | category | flops | bytes accessed | tf_op | source)
XLA Modules:
  0.0 89.3 jit_solution(8976678175062276426)
XLA Ops:
  0.0 0.0 copy-start
  0.0 1.4 %copy-done = bf16[256,3072]{1,0:T(8,128)(2,1)S(1)} copy-done((bf16[256,3072]{1,0:T(8,128)(2,1)S(1)}, bf16[256,3072]{1,0:T(8,128)(2,1)}, u32[]{:S(2)}) %copy-start) | copy-done | bytes 1572888
  1.4 0.0 copy-start.1
  1.4 0.9 %copy-done.1 = bf16[256,256]{1,0:T(8,128)(2,1)S(1)} copy-done((bf16[256,256]{1,0:T(8,128)(2,1)S(1)}, bf16[256,256]{1,0:T(8,128)(2,1)}, u32[]{:S(2)}) %copy-start.1) | copy-done | bytes 131096
  2.3 0.0 copy-start.2
  2.3 0.9 %copy-done.2 = bf16[256,256]{1,0:T(8,128)(2,1)S(1)} copy-done((bf16[256,256]{1,0:T(8,128)(2,1)S(1)}, bf16[256,256]{1,0:T(8,128)(2,1)}, u32[]{:S(2)}) %copy-start.2) | copy-done | bytes 131096
  3.2 0.0 copy-start.3
  3.2 0.9 %copy-done.3 = bf16[256,256]{1,0:T(8,128)(2,1)S(1)} copy-done((bf16[256,256]{1,0:T(8,128)(2,1)S(1)}, bf16[256,256]{1,0:T(8,128)(2,1)}, u32[]{:S(2)}) %copy-start.3) | copy-done | bytes 131096
  4.1 0.0 copy-start.4
  4.1 0.7 copy-done.4
  4.8 0.0 copy-start.5
  4.8 0.7 copy-done.5
  5.5 83.2 %shard_map.64 = bf16[32,3072]{1,0:T(8,128)(2,1)S(1)} custom-call(s32[32]{0:T(128)S(1)} %copy-done.5, s32[256]{0:T(256)S(1)} %copy-done.4, bf16[8,2,16,256]{3,2,1,0:T(8,128)(2,1)S(1)} %bitcast.1, bf16[256,256]{1,0:T(8,128)(2,1)S(1)} %copy-done.2, bf16[256,256]{1,0:T(8,128)(2,1)S(1)} %copy-done.3, bf16[256,3072]{1,0:T(8,128)(2,1)S(1)} %copy-done), custom_call_target="tpu_custom_call" | custom-call | flops 8999999488 | bytes 6000000 | tf_op jit(solution)/shard_map/pallas_call | solution.py:309
  88.6 0.7 copy.8
Async XLA Ops:
  0.0 1.4 %copy-start = (bf16[256,3072]{1,0:T(8,128)(2,1)S(1)}, bf16[256,3072]{1,0:T(8,128)(2,1)}, u32[]{:S(2)}) copy-start(bf16[256,3072]{1,0:T(8,128)(2,1)} %w_in.1) | copy-start | bytes 4718596
  1.4 0.9 %copy-start.1 = (bf16[256,256]{1,0:T(8,128)(2,1)S(1)}, bf16[256,256]{1,0:T(8,128)(2,1)}, u32[]{:S(2)}) copy-start(bf16[256,256]{1,0:T(8,128)(2,1)} %param.6) | copy-start | bytes 393220
  2.3 0.9 %copy-start.2 = (bf16[256,256]{1,0:T(8,128)(2,1)S(1)}, bf16[256,256]{1,0:T(8,128)(2,1)}, u32[]{:S(2)}) copy-start(bf16[256,256]{1,0:T(8,128)(2,1)} %k_in.1) | copy-start | bytes 393220
  3.2 0.9 %copy-start.3 = (bf16[256,256]{1,0:T(8,128)(2,1)S(1)}, bf16[256,256]{1,0:T(8,128)(2,1)}, u32[]{:S(2)}) copy-start(bf16[256,256]{1,0:T(8,128)(2,1)} %v_in.1) | copy-start | bytes 393220
  4.1 0.7 copy-start.4
  4.8 0.7 copy-start.5

commit v2 on v1

v2 whole, which is shorter than its diff:
```python
import functools

import jax
import jax.numpy as jnp
from jax import lax
from jax.experimental import pallas as pl
from jax.experimental.pallas import tpu as pltpu
from jax.sharding import PartitionSpec as P

HD = 128
SLICE = 64
NX, NY, NZ = 4, 8, 8
ROWS = 256
PIECE = 128
KEYS = NX * 2 * ROWS
D = 3072
HIDDEN = -1e30
LOG2E = 1.4426950408889634
SCALE = HD**-0.5 * LOG2E
MESH = pl.DeviceIdType.MESH


def kernel(
    lens, disp, q_in, k_in, v_in, w_in, out,
    qbuf, qbias, kbuf, vbuf, vt, konehot, score_a, score_b, peak_a, peak_b,
    part_o, part_l, yo_send, yl_send, yo_recv, yl_recv, att, att_send, wbuf, proj, z_send, z_recv,
    loc_sem, sib_s, sib_r, q_s, q_r, kv_s, kv_r, yo_s, yo_r, yl_s, yl_r, at_s, at_r, z_s, z_r,
):
    ctx, z = lax.axis_index("ctx"), lax.axis_index("head")
    c = lax.rem(ctx, 2)
    x = lax.rem(ctx // 2, NX)
    y = ctx // (2 * NX)

    def at(yy, xx, cc, zz):
        return ((yy * NX + xx) * 2 + cc, zz)

    def ring(i, step, size):
        return lax.rem(i + step + size, size)

    sibling = at(y, x, 1 - c, z)

    def y_dev(step):
        return at(ring(y, step, NY), x, c, z)

    def x_dev(step):
        return at(y, ring(x, step, NX), c, z)

    def z_dev(step):
        return at(y, x, c, ring(z, step, NZ))

    partners = [sibling, y_dev(4)] + [f(s) for f in (x_dev, y_dev, z_dev) for s in (-1, 1)]
    barrier = pltpu.get_barrier_semaphore()
    for dev in partners:
        pl.semaphore_signal(barrier, inc=1, device_id=dev, device_id_type=MESH)

    mine = pl.ds(pl.multiple_of(c * HD, HD), HD)
    other = pl.ds(pl.multiple_of((1 - c) * HD, HD), HD)
    local = [
        pltpu.make_async_copy(q_in.at[:, p, :, mine], qbuf.at[0, p, c], loc_sem.at[p])
        for p in range(2)
    ]
    local.append(pltpu.make_async_copy(k_in.at[:, mine], kbuf.at[0, c], loc_sem.at[2]))
    local.append(pltpu.make_async_copy(v_in.at[:, mine], vbuf.at[0, c], loc_sem.at[3]))
    load_w = pltpu.make_async_copy(w_in, wbuf, loc_sem.at[4])
    for copy in local:
        copy.start()
    pl.semaphore_wait(barrier, len(partners))

    sent = []

    def send(src, dst, s, r, dev):
        copy = pltpu.make_async_remote_copy(
            src_ref=src, dst_ref=dst, send_sem=s, recv_sem=r, device_id=dev, device_id_type=MESH
        )
        copy.start()
        sent.append(copy)
        return copy

    swaps = [
        send(k_in.at[:, other], kbuf.at[0, c], sib_s.at[2], sib_r.at[2], sibling),
        send(v_in.at[:, other], vbuf.at[0, c], sib_s.at[3], sib_r.at[3], sibling),
    ] + [
        send(q_in.at[:, p, :, other], qbuf.at[0, p, c], sib_s.at[p], sib_r.at[p], sibling)
        for p in range(2)
    ]
    for copy in local:
        copy.wait()
    for copy in swaps:
        copy.wait_recv()

    def q_send(slot, block, step, piece):
        there = (block - step) % NY
        return send(
            qbuf.at[block, piece], qbuf.at[there, piece], q_s.at[slot], q_r.at[slot], y_dev(step)
        )

    def kv_send(slot, ref, block, step):
        there = (block - step) % NX
        return send(ref.at[block], ref.at[there], kv_s.at[slot], kv_r.at[slot], x_dev(step))

    k_right = kv_send(0, kbuf, 0, 1)
    v_left = kv_send(1, vbuf, 0, -1)
    hop = {}
    for p in range(2):
        for w in range(2):
            hop[1, p, w] = q_send(2 * p + w, 0, 1 - 2 * w, p)
    v_right = kv_send(2, vbuf, 0, 1)
    k_left = kv_send(3, kbuf, 0, -1)
    across = [q_send(12 + p, 0, 4, p) for p in range(2)]
    load_w.start()

    lane = lax.broadcasted_iota(jnp.int32, (1, HD), 1)

    def bounds(g, carry):
        total, first, last = carry
        after = total + lens[g]
        return after, jnp.where(lane == g, total, first), jnp.where(lane == g, after, last)

    _, first, last = lax.fori_loop(
        0, 32, bounds,
        (jnp.int32(0), jnp.full((1, HD), -1, jnp.int32), jnp.zeros((1, HD), jnp.int32)),
    )
    sub64 = lax.broadcasted_iota(jnp.int32, (SLICE, HD), 0)
    sub16 = lax.broadcasted_iota(jnp.int32, (16, HD), 0)

    def key_marks(s, _):
        block = ring(x, s // 8, NX)
        pos = disp[(y * NX + block) * 8 + lax.rem(s, 8)] * SLICE + sub64
        inside = jnp.where((first <= pos) & (pos < last), 1.0, 0.0)
        konehot[pl.ds(pl.multiple_of(s * SLICE, SLICE), SLICE), :] = inside.astype(jnp.bfloat16)
        return 0

    lax.fori_loop(0, KEYS // SLICE, key_marks, 0)

    def query_marks(i, _):
        owner, half, s = i // 8, lax.rem(i // 4, 2), lax.rem(i, 4)
        start = disp[(ring(y, owner, NY) * NX + x) * 8 + half * 4 + s] * SLICE
        for j in range(2):
            for p in range(2):
                pos = start + (j * 32 + p * 16) + sub16
                qbias[owner, p, half, 2 * s + j] = jnp.where(first > pos, HIDDEN, 0.0).astype(
                    jnp.bfloat16
                )
        return 0

    def turn(b):
        block = vbuf[b].reshape(512, HD).astype(jnp.float32)
        vt[:HD, b * 512 : (b + 1) * 512] = jnp.transpose(block).astype(jnp.bfloat16)

    vt[HD:, :] = jnp.ones((16, KEYS), jnp.bfloat16)
    turn(0)

    def forward(d, p):
        for w in range(2):
            hop[d - 1, p, w].wait_recv()
            way = 1 - 2 * w
            hop[d, p, w] = q_send(4 * (d - 1) + 2 * p + w, -way * (d - 1) % NY, way, p)

    k_right.wait_recv()
    k_far = kv_send(4, kbuf, 3, 1)
    v_left.wait_recv()
    v_far = kv_send(5, vbuf, 1, -1)
    forward(2, 0)
    forward(2, 1)
    lax.fori_loop(0, NY * 8, query_marks, 0)
    turn(1)
    v_right.wait_recv()
    turn(3)
    k_left.wait_recv()
    forward(3, 0)
    forward(3, 1)
    k_far.wait_recv()
    for copy in across:
        copy.wait_recv()

    def unit(u):
        p = u % 2
        group = (u + 2) // 4
        short = (u + 2) % 4 // 2
        return ((2 * p - 1) * (1 - 2 * short) * (4 - group) + NY) % NY, p

    def scores(u, score, peak_ref):
        owner, p = unit(u)
        qa = jnp.concatenate(
            [qbuf[owner, p].reshape(ROWS, HD), qbias[owner, p].reshape(ROWS, HD)], axis=1
        )
        peak = None
        for b in range(NX):
            cut = slice(b * 512, (b + 1) * 512)
            ka = jnp.concatenate([kbuf[b].reshape(512, HD), konehot[cut, :]], axis=1)
            s = lax.dot_general(
                ka, qa, (((1,), (1,)), ((), ())), preferred_element_type=jnp.float32
            )
            score[cut, :] = s
            tile = jnp.max(s.reshape(64, 8, ROWS), axis=0)
            peak = tile if peak is None else jnp.maximum(peak, tile)
            if b == NX - 1:
                peak_ref[...] = jnp.broadcast_to(jnp.max(peak, axis=0, keepdims=True), (8, ROWS))
            yield

    def weigh(u, score, peak_ref):
        owner, p = unit(u)
        peak = peak_ref[0:1, :]
        total = None
        for b in range(NX):
            cut = slice(b * 512, (b + 1) * 512)
            w = jnp.exp2((score[cut, :] - peak) * SCALE).astype(jnp.bfloat16)
            t = jnp.dot(vt[:, cut], w, preferred_element_type=jnp.float32)
            total = t if total is None else total + t
            if b == NX - 1:
                weight = total[HD : HD + 1, :]
                part_o[owner, p] = total[:HD, :] / weight
                part_l[owner, p] = jnp.broadcast_to(
                    jnp.log2(weight) + peak * SCALE, (8, ROWS)
                )
            yield

    def beside(*streams):
        for _ in range(NX):
            for stream in streams:
                next(stream)

    a, b = (score_a, peak_a), (score_b, peak_b)

    def pair(u, more):
        beside(scores(u + 1, *b), weigh(u, *a))
        if more:
            beside(scores(u + 2, *a), weigh(u + 1, *b))
        else:
            beside(weigh(u + 1, *b))

    def merge(o, l, slot):
        m = yl_recv[slot][0:1, :]
        top = jnp.maximum(l, m)
        wa, wb = jnp.exp2(l - top), jnp.exp2(m - top)
        total = wa + wb
        o = o * (wa / total) + yo_recv[slot].astype(jnp.float32) * (wb / total)
        return o, top + jnp.log2(total)

    def y_send(slot, o, l, dev):
        yo_send[slot] = o.astype(jnp.bfloat16)
        yl_send[slot] = jnp.broadcast_to(l, (8, ROWS))
        return (
            send(yo_send.at[slot], yo_recv.at[slot], yo_s.at[slot], yo_r.at[slot], dev),
            send(yl_send.at[slot], yl_recv.at[slot], yl_s.at[slot], yl_r.at[slot], dev),
        )

    yhops = {}

    def y_step(j):
        for short in range(2):
            for p in range(2):
                if short and j == 1:
                    continue
                travel = (2 * p - 1) * (1 - 2 * short)
                owner = travel * (5 - j) % NY
                o, l = part_o[owner, p], part_l[owner, p][0:1, :]
                slot = p * 7 + (2 + j if short else j - 1)
                if j > 1 + short:
                    for copy in yhops[slot - 1]:
                        copy.wait_recv()
                    o, l = merge(o, l, slot - 1)
                yhops[slot] = y_send(slot, o, l, y_dev(travel))

    beside(scores(0, *a))
    v_far.wait_recv()
    turn(2)
    pair(0, False)
    y_step(1)
    for p in range(2):
        for w in range(2):
            hop[3, p, w].wait_recv()
    beside(scores(2, *a))
    for j in range(2, 5):

        def two(i, _):
            pair(4 * j - 6 + 2 * i, True)
            return 0

        lax.fori_loop(0, 2, two, 0)
        y_step(j)
    pair(14, False)

    swaps = []
    for p in range(2):
        o, l = part_o[0, p], part_l[0, p][0:1, :]
        for slot in (p * 7 + 6, p * 7 + 3):
            for copy in yhops[slot]:
                copy.wait_recv()
            o, l = merge(o, l, slot)
        o = jnp.transpose(o).astype(jnp.bfloat16)
        att_send[p] = jnp.where(c == 0, o[PIECE:], o[:PIECE])
        swaps.append(send(att_send.at[p], att.at[p, c], at_s.at[p], at_r.at[p], sibling))
        att[p, c] = jnp.where(c == 0, o[:PIECE], o[PIECE:])

    load_w.wait()

    def project(p):
        rows = jnp.concatenate([att[p, 0], att[p, 1]], axis=1)

        def columns(n, _):
            cut = pl.ds(pl.multiple_of(n * 768, 768), 768)
            r = jnp.dot(rows, wbuf[:, cut], preferred_element_type=jnp.float32)
            proj[p, :, :, cut] = r.reshape(NZ, 16, 768)
            return 0

        lax.fori_loop(0, D // 768, columns, 0)

    zhops = {}
    for j in range(1, 5):
        for short in range(2):
            for p in range(2):
                if short and j == 1:
                    continue
                if j == 1:
                    swaps[p].wait_recv()
                    project(p)
                travel = (2 * p - 1) * (1 - 2 * short)
                r = proj[p, ring(z, travel * (5 - j), NZ)]
                slot = p * 7 + (2 + j if short else j - 1)
                if j > 1 + short:
                    zhops[slot - 1].wait_recv()
                    r = r + z_recv[slot - 1].astype(jnp.float32)
                z_send[slot] = r.astype(jnp.bfloat16)
                zhops[slot] = send(
                    z_send.at[slot], z_recv.at[slot], z_s.at[slot], z_r.at[slot], z_dev(travel)
                )
    for p in range(2):
        r = proj[p, z]
        for slot in (p * 7 + 6, p * 7 + 3):
            zhops[slot].wait_recv()
            r = r + z_recv[slot].astype(jnp.float32)
        out[p * 16 : (p + 1) * 16, :] = r.astype(jnp.bfloat16)
    for copy in sent:
        copy.wait_send()


def body(queries, keys, values, group_lens, dispatch, out_weight):
    bf, f32 = jnp.bfloat16, jnp.float32
    dma = pltpu.SemaphoreType.DMA
    anywhere = pl.BlockSpec(memory_space=pl.ANY)
    smem = pl.BlockSpec(memory_space=pltpu.SMEM)
    return pl.pallas_call(
        kernel,
        out_shape=jax.ShapeDtypeStruct((ROWS // NZ, D), bf),
        in_specs=[smem, smem, anywhere, anywhere, anywhere, anywhere],
        out_specs=pl.BlockSpec(memory_space=pltpu.VMEM),
        scratch_shapes=[
            pltpu.VMEM((NY, 2, 2, NZ, 16, HD), bf),
            pltpu.VMEM((NY, 2, 2, NZ, 16, HD), bf),
            pltpu.VMEM((NX, 2, ROWS, HD), bf),
            pltpu.VMEM((NX, 2, ROWS, HD), bf),
            pltpu.VMEM((HD + 16, KEYS), bf),
            pltpu.VMEM((KEYS, HD), bf),
            pltpu.VMEM((KEYS, ROWS), f32),
            pltpu.VMEM((KEYS, ROWS), f32),
            pltpu.VMEM((8, ROWS), f32),
            pltpu.VMEM((8, ROWS), f32),
            pltpu.VMEM((NY, 2, HD, ROWS), f32),
            pltpu.VMEM((NY, 2, 8, ROWS), f32),
            pltpu.VMEM((14, HD, ROWS), bf),
            pltpu.VMEM((14, 8, ROWS), f32),
            pltpu.VMEM((14, HD, ROWS), bf),
            pltpu.VMEM((14, 8, ROWS), f32),
            pltpu.VMEM((2, 2, PIECE, HD), bf),
            pltpu.VMEM((2, PIECE, HD), bf),
            pltpu.VMEM((2 * HD, D), bf),
            pltpu.VMEM((2, NZ, 16, D), f32),
            pltpu.VMEM((14, 16, D), bf),
            pltpu.VMEM((14, 16, D), bf),
            dma((5,)), dma((4,)), dma((4,)), dma((14,)), dma((14,)), dma((6,)), dma((6,)),
            dma((14,)), dma((14,)), dma((14,)), dma((14,)), dma((2,)), dma((2,)),
            dma((14,)), dma((14,)),
        ],
        compiler_params=pltpu.CompilerParams(
            collective_id=0, has_side_effects=True, vmem_limit_bytes=60 * 1024 * 1024
        ),
        cost_estimate=pl.CostEstimate(
            flops=9_000_000_000, bytes_accessed=6_000_000, transcendentals=8_400_000
        ),
    )(
        group_lens,
        dispatch,
        queries.reshape(NZ, 2, 16, 2 * HD),
        keys,
        values,
        out_weight,
    )


def solution(mesh):
    return jax.shard_map(
        body,
        mesh=mesh,
        in_specs=(P("ctx", "head"), P("ctx", "head"), P("ctx", "head"), P(), P(), P("head", None)),
        out_specs=P(("ctx", "head"), None),
        check_vma=False,
    )
```

time: 89.5 us -> 75.5 us (0.84)
  the two profiles are of different devices: /device:TPU:8 before, /device:TPU:1 now
where the time goes in v2:
time: 75.5 us; the launch traced here: 75.3 us
  Pallas kernels  73.6 us (97%)
  local copies, waits for them, and re-layouts  1.62 us (2%)
    pallas_call x1, Pallas kernels, body(): pl.pallas_call(kernel, out_shape=jax.ShapeDtypeStruct((ROWS // NZ, D), bf...  73.6 us
    unnamed x1, local copies, waits for them, and re-layouts  1.62 us

profile of v2, /device:TPU:1, one launch (start us, length us, event | category | flops | bytes accessed | tf_op | source)
XLA Modules:
  0.0 75.3 jit_solution(11513300807985269526)
XLA Ops:
  0.0 73.6 %shard_map.64 = bf16[32,3072]{1,0:T(8,128)(2,1)} custom-call(s32[32]{0:T(128)} %lens.1, s32[256]{0:T(256)} %disp.1, bf16[8,2,16,256]{3,2,1,0:T(8,128)(2,1)} %bitcast.1, bf16[256,256]{1,0:T(8,128)(2,1)} %k_in.1, bf16[256,256]{1,0:T(8,128)(2,1)} %v_in.1, bf16[256,3072]{1,0:T(8,128)(2,1)} %w_in.1), custom_call_target="tpu_custom_call" | custom-call | flops 8999999488 | bytes 6000000 | tf_op jit(solution)/shard_map/pallas_call | solution.py:343
  73.7 1.6 %copy.8 = bf16[32,3072]{1,0:T(8,128)(2,1)} copy(bf16[32,3072]{1,0:T(8,128)(2,1)} %shard_map.64) | data formatting | bytes 393216

commit v3 on v2

v3 whole, which is shorter than its diff:
```python
import functools

import jax
import jax.numpy as jnp
from jax import lax
from jax.experimental import pallas as pl
from jax.experimental.pallas import tpu as pltpu
from jax.sharding import PartitionSpec as P

HD = 128
SLICE = 64
NX, NY, NZ = 4, 8, 8
ROWS = 256
PIECE = 128
KEYS = NY * 2 * ROWS
D = 3072
HIDDEN = -1e30
LOG2E = 1.4426950408889634
SCALE = HD**-0.5 * LOG2E
MESH = pl.DeviceIdType.MESH


def kernel(
    lens_in, disp_in, q_in, k_in, v_in, w_in, out,
    lens, disp, qbuf, qbias, kbuf, vbuf, vt, konehot, score_a, score_b, peak_a, peak_b,
    part_o, part_m, part_l, yo_send, yl_send, yo_recv, yl_recv, att, att_send, wbuf, proj, z_send, z_recv,
    loc_sem, sib_s, sib_r, q_s, q_r, kv_s, kv_r, yo_s, yo_r, yl_s, yl_r, at_s, at_r, z_s, z_r,
):
    ctx, z = lax.axis_index("ctx"), lax.axis_index("head")
    c = lax.rem(ctx, 2)
    x = lax.rem(ctx // 2, NX)
    y = ctx // (2 * NX)

    def at(yy, xx, cc, zz):
        return ((yy * NX + xx) * 2 + cc, zz)

    def ring(i, step, size):
        return lax.rem(i + step + size, size)

    sibling = at(y, x, 1 - c, z)

    def y_dev(step, core=c):
        return at(ring(y, step, NY), x, core, z)

    def x_dev(step, core=c):
        return at(y, ring(x, step, NX), core, z)

    def z_dev(step):
        return at(y, x, c, ring(z, step, NZ))

    partners = [sibling, x_dev(2), z_dev(-1), z_dev(1)]
    partners += [f(s, core) for f in (x_dev, y_dev) for s in (-1, 1) for core in (c, 1 - c)]
    barrier = pltpu.get_barrier_semaphore()
    for dev in partners:
        pl.semaphore_signal(barrier, inc=1, device_id=dev, device_id_type=MESH)

    mine = pl.ds(pl.multiple_of(c * HD, HD), HD)
    other = pl.ds(pl.multiple_of((1 - c) * HD, HD), HD)
    local = [
        pltpu.make_async_copy(q_in.at[:, p, :, mine], qbuf.at[0, p, c], loc_sem.at[p])
        for p in range(2)
    ]
    local.append(pltpu.make_async_copy(k_in.at[:, mine], kbuf.at[0, c], loc_sem.at[2]))
    local.append(pltpu.make_async_copy(v_in.at[:, mine], vbuf.at[0, c], loc_sem.at[3]))
    local.append(pltpu.make_async_copy(lens_in, lens, loc_sem.at[4]))
    local.append(pltpu.make_async_copy(disp_in, disp, loc_sem.at[5]))
    load_w = pltpu.make_async_copy(w_in, wbuf, loc_sem.at[6])
    for copy in local:
        copy.start()
    pl.semaphore_wait(barrier, len(partners))

    sent = []

    def drain():
        while sent:
            sent.pop(0).wait_send()

    def send(src, dst, s, r, dev):
        copy = pltpu.make_async_remote_copy(
            src_ref=src, dst_ref=dst, send_sem=s, recv_sem=r, device_id=dev, device_id_type=MESH
        )
        copy.start()
        sent.append(copy)
        return copy

    halves = (c, 1 - c)
    lanes = (mine, other)

    def q_first(p, w):
        way = 1 - 2 * w
        return [
            send(
                q_in.at[:, p, :, lanes[t]], qbuf.at[-way % NX, p, c],
                q_s.at[4 * p + 2 * w + t], q_r.at[4 * p + 2 * w + t], x_dev(way, halves[t]),
            )
            for t in range(2)
        ]

    sources, blocks = (k_in, v_in), (kbuf, vbuf)
    hop = {}

    def kv_first(kind):
        for t in range(2):
            for w in range(2):
                way = 1 - 2 * w
                slot = 4 * kind + 2 * w + t
                hop[1, kind, w, t] = send(
                    sources[kind].at[:, lanes[t]], blocks[kind].at[-way % NY, c],
                    kv_s.at[slot], kv_r.at[slot], y_dev(way, halves[t]),
                )

    kv_first(0)
    q_hop = {(p, w): q_first(p, w) for p in range(2) for w in range(2)}
    swaps = [
        send(k_in.at[:, other], kbuf.at[0, c], sib_s.at[2], sib_r.at[2], sibling),
        send(v_in.at[:, other], vbuf.at[0, c], sib_s.at[3], sib_r.at[3], sibling),
    ] + [
        send(q_in.at[:, p, :, other], qbuf.at[0, p, c], sib_s.at[p], sib_r.at[p], sibling)
        for p in range(2)
    ]
    kv_first(1)

    def arrive(d, kind, w, t):
        hop[d, kind, w, t].wait_recv()
        if d == 4 or (d == 3 and kind != w):
            return
        way = 1 - 2 * w
        here, there = -way * d % NY, -way * (d + 1) % NY
        slot = 8 * d + 4 * kind + 2 * w + t if d < 3 else 24 + 2 * kind + t
        ref = blocks[kind]
        hop[d + 1, kind, w, t] = send(
            ref.at[here, halves[t]], ref.at[there, halves[t]],
            kv_s.at[slot], kv_r.at[slot], y_dev(way),
        )

    def arrivals(d):
        if d == 4:
            return [(d, kind, kind, t) for kind in range(2) for t in range(2)]
        return [(d, kind, w, t) for kind in range(2) for t in range(2) for w in range(2)]

    load_w.start()

    for copy in local:
        copy.wait()
    lane = lax.broadcasted_iota(jnp.int32, (1, HD), 1)

    def bounds(g, carry):
        total, first, last = carry
        after = total + lens[g]
        return after, jnp.where(lane == g, total, first), jnp.where(lane == g, after, last)

    _, first, last = lax.fori_loop(
        0, 32, bounds,
        (jnp.int32(0), jnp.full((1, HD), -1, jnp.int32), jnp.zeros((1, HD), jnp.int32)),
    )
    sub64 = lax.broadcasted_iota(jnp.int32, (SLICE, HD), 0)
    sub16 = lax.broadcasted_iota(jnp.int32, (16, HD), 0)

    def key_marks(s, _):
        block = ring(y, s // 8, NY)
        pos = disp[(block * NX + x) * 8 + lax.rem(s, 8)] * SLICE + sub64
        inside = jnp.where((first <= pos) & (pos < last), 1.0, 0.0)
        konehot[pl.ds(pl.multiple_of(s * SLICE, SLICE), SLICE), :] = inside.astype(jnp.bfloat16)
        return 0

    lax.fori_loop(0, KEYS // SLICE, key_marks, 0)

    def query_marks(i, _):
        owner, half, s = i // 8, lax.rem(i // 4, 2), lax.rem(i, 4)
        start = disp[(y * NX + ring(x, owner, NX)) * 8 + half * 4 + s] * SLICE
        for j in range(2):
            for p in range(2):
                pos = start + (j * 32 + p * 16) + sub16
                qbias[owner, p, half, 2 * s + j] = jnp.where(first > pos, HIDDEN, 0.0).astype(
                    jnp.bfloat16
                )
        return 0

    def turn(b):
        block = vbuf[b].reshape(512, HD).astype(jnp.float32)
        vt[:HD, b * 512 : (b + 1) * 512] = jnp.transpose(block).astype(jnp.bfloat16)

    vt[HD:, :] = jnp.ones((16, KEYS), jnp.bfloat16)

    lax.fori_loop(0, NX * 8, query_marks, 0)
    for copy in swaps:
        copy.wait_recv()
    turn(0)

    def level_blocks(d):
        return (d,) if d in (0, 4) else (d, NY - d)

    def scores(d, owner, p, score, peak_ref):
        qa = jnp.concatenate(
            [qbuf[owner, p].reshape(ROWS, HD), qbias[owner, p].reshape(ROWS, HD)], axis=1
        )
        peak = None
        for i, b in enumerate(level_blocks(d)):
            ka = jnp.concatenate(
                [kbuf[b].reshape(512, HD), konehot[b * 512 : (b + 1) * 512, :]], axis=1
            )
            s = lax.dot_general(
                ka, qa, (((1,), (1,)), ((), ())), preferred_element_type=jnp.float32
            )
            score[i * 512 : (i + 1) * 512, :] = s
            tile = jnp.max(s.reshape(64, 8, ROWS), axis=0)
            peak = tile if peak is None else jnp.maximum(peak, tile)
            if b == level_blocks(d)[-1]:
                peak_ref[...] = jnp.broadcast_to(jnp.max(peak, axis=0, keepdims=True), (8, ROWS))
            yield

    def weigh(d, owner, p, score, peak_ref):
        peak = peak_ref[0:1, :]
        if d > 0:
            before = part_m[owner, p][0:1, :]
            peak = jnp.maximum(before, peak)
        total = None
        for i, b in enumerate(level_blocks(d)):
            w = jnp.exp2((score[i * 512 : (i + 1) * 512, :] - peak) * SCALE).astype(jnp.bfloat16)
            t = jnp.dot(
                vt[:, b * 512 : (b + 1) * 512], w, preferred_element_type=jnp.float32
            )
            total = t if total is None else total + t
            if b == level_blocks(d)[-1]:
                o, l = total[:HD, :], total[HD : HD + 1, :]
                if d > 0:
                    factor = jnp.exp2((before - peak) * SCALE)
                    o = part_o[owner, p] * factor + o
                    l = part_l[owner, p][0:1, :] * factor + l
                if d < 4 or owner == 0:
                    part_o[owner, p] = o
                    part_m[owner, p] = jnp.broadcast_to(peak, (8, ROWS))
                    part_l[owner, p] = jnp.broadcast_to(l, (8, ROWS))
                else:
                    give(owner, p, o, peak, l)
            yield

    def beside(*streams):
        live = list(streams)
        while live:
            live = [stream for stream in live if next(stream, True) is None]

    sub8 = lax.broadcasted_iota(jnp.int32, (8, ROWS), 0)
    given = {}

    def give(owner, p, o, peak, l):
        slot = 3 * p + owner - 1
        yo_send[slot] = o.astype(jnp.bfloat16)
        yl_send[slot] = jnp.where(sub8 < 4, peak, l)
        dev = x_dev(owner)
        given[slot] = (
            send(yo_send.at[slot], yo_recv.at[slot], yo_s.at[slot], yo_r.at[slot], dev),
            send(yl_send.at[slot], yl_recv.at[slot], yl_s.at[slot], yl_r.at[slot], dev),
        )

    buffers = ((score_a, peak_a), (score_b, peak_b))

    def stage(d, units, tasks):
        beside(scores(d, *units[0], *buffers[0]))
        for i, unit in enumerate(units):
            for task in tasks[i : i + 1]:
                arrive(*task)
            streams = [weigh(d, *unit, *buffers[i % 2])]
            if i + 1 < len(units):
                streams.insert(0, scores(d, *units[i + 1], *buffers[(i + 1) % 2]))
            beside(*streams)
        for task in tasks[len(units) :]:
            arrive(*task)

    order = [(owner, p) for owner in (2, 1, 3, 0) for p in range(2)]
    stage(0, order[6:], [])
    q_far = []
    for t in range(2):
        for p in range(2):
            q_hop[p, p][t].wait_recv()
            way = 1 - 2 * p
            slot = 8 + 2 * p + t
            q_far.append(
                send(
                    qbuf.at[-way % NX, p, halves[t]], qbuf.at[2, p, halves[t]],
                    q_s.at[slot], q_r.at[slot], x_dev(way),
                )
            )
    for task in arrivals(1)[:2]:
        arrive(*task)
    for p in range(2):
        for copy in q_hop[p, 1 - p]:
            copy.wait_recv()
    stage(0, order[2:6], arrivals(1)[2:])
    for copy in q_far:
        copy.wait_recv()
    stage(0, order[:2], [])
    for d in range(1, 4):
        if d == 3:
            drain()
        turn(d)
        turn(NY - d)
        stage(d, order, arrivals(d + 1))
    turn(4)
    stage(4, order, [])

    swaps = []
    for p in range(2):
        slots = [3 * p + k for k in range(3)]
        for slot in slots:
            for copy in given[slot]:
                copy.wait_recv()
        tops = [part_m[0, p][0:1, :]] + [yl_recv[slot][0:1, :] for slot in slots]
        sums = [part_l[0, p][0:1, :]] + [yl_recv[slot][4:5, :] for slot in slots]
        top = functools.reduce(jnp.maximum, tops)
        factors = [jnp.exp2((m - top) * SCALE) for m in tops]
        inverse = 1.0 / sum(f * l for f, l in zip(factors, sums))
        o = part_o[0, p] * (factors[0] * inverse)
        for f, slot in zip(factors[1:], slots):
            o = o + yo_recv[slot].astype(jnp.float32) * (f * inverse)
        o = jnp.transpose(o).astype(jnp.bfloat16)
        att_send[p] = jnp.where(c == 0, o[PIECE:], o[:PIECE])
        swaps.append(send(att_send.at[p], att.at[p, c], at_s.at[p], at_r.at[p], sibling))
        att[p, c] = jnp.where(c == 0, o[:PIECE], o[PIECE:])

    load_w.wait()

    def project(p):
        rows = jnp.concatenate([att[p, 0], att[p, 1]], axis=1)

        def columns(n, _):
            cut = pl.ds(pl.multiple_of(n * 768, 768), 768)
            r = jnp.dot(rows, wbuf[:, cut], preferred_element_type=jnp.float32)
            proj[p, :, :, cut] = r.reshape(NZ, 16, 768)
            return 0

        lax.fori_loop(0, D // 768, columns, 0)

    zhops = {}
    half = D // 2
    for j in range(1, 5):
        if j == 3:
            drain()
        for short in range(2):
            for p in range(2):
                if short and j == 4:
                    continue
                if j == 1 and not short:
                    swaps[p].wait_recv()
                    project(p)
                for h in range(2):
                    travel = (2 * p - 1) * (1 - 2 * short) * (1 - 2 * h)
                    owner = ring(z, travel * (5 - j - short), NZ)
                    r = proj[p, owner, :, h * half : (h + 1) * half]
                    slot = (2 * p + h) * 7 + 4 * short + j - 1
                    if j > 1:
                        zhops[slot - 1].wait_recv()
                        r = r + z_recv[slot - 1].astype(jnp.float32)
                    z_send[slot] = r.astype(jnp.bfloat16)
                    zhops[slot] = send(
                        z_send.at[slot], z_recv.at[slot], z_s.at[slot], z_r.at[slot], z_dev(travel)
                    )
    for p in range(2):
        for h in range(2):
            r = proj[p, z, :, h * half : (h + 1) * half]
            for slot in ((2 * p + h) * 7 + 6, (2 * p + h) * 7 + 3):
                zhops[slot].wait_recv()
                r = r + z_recv[slot].astype(jnp.float32)
            out[p * 16 : (p + 1) * 16, h * half : (h + 1) * half] = r.astype(jnp.bfloat16)
    drain()


def body(queries, keys, values, group_lens, dispatch, out_weight):
    bf, f32 = jnp.bfloat16, jnp.float32
    dma = pltpu.SemaphoreType.DMA
    anywhere = pl.BlockSpec(memory_space=pl.ANY)
    return pl.pallas_call(
        kernel,
        out_shape=jax.ShapeDtypeStruct((ROWS // NZ, D), bf),
        in_specs=[anywhere] * 6,
        out_specs=pl.BlockSpec(memory_space=pltpu.VMEM),
        scratch_shapes=[
            pltpu.SMEM((32,), jnp.int32),
            pltpu.SMEM((256,), jnp.int32),
            pltpu.VMEM((NX, 2, 2, NZ, 16, HD), bf),
            pltpu.VMEM((NX, 2, 2, NZ, 16, HD), bf),
            pltpu.VMEM((NY, 2, ROWS, HD), bf),
            pltpu.VMEM((NY, 2, ROWS, HD), bf),
            pltpu.VMEM((HD + 16, KEYS), bf),
            pltpu.VMEM((KEYS, HD), bf),
            pltpu.VMEM((1024, ROWS), f32),
            pltpu.VMEM((1024, ROWS), f32),
            pltpu.VMEM((8, ROWS), f32),
            pltpu.VMEM((8, ROWS), f32),
            pltpu.VMEM((NX, 2, HD, ROWS), f32),
            pltpu.VMEM((NX, 2, 8, ROWS), f32),
            pltpu.VMEM((NX, 2, 8, ROWS), f32),
            pltpu.VMEM((6, HD, ROWS), bf),
            pltpu.VMEM((6, 8, ROWS), f32),
            pltpu.VMEM((6, HD, ROWS), bf),
            pltpu.VMEM((6, 8, ROWS), f32),
            pltpu.VMEM((2, 2, PIECE, HD), bf),
            pltpu.VMEM((2, PIECE, HD), bf),
            pltpu.VMEM((2 * HD, D), bf),
            pltpu.VMEM((2, NZ, 16, D), f32),
            pltpu.VMEM((28, 16, D // 2), bf),
            pltpu.VMEM((28, 16, D // 2), bf),
            dma((7,)), dma((4,)), dma((4,)), dma((12,)), dma((12,)), dma((28,)), dma((28,)),
            dma((6,)), dma((6,)), dma((6,)), dma((6,)), dma((2,)), dma((2,)),
            dma((28,)), dma((28,)),
        ],
        compiler_params=pltpu.CompilerParams(
            collective_id=0, has_side_effects=True, vmem_limit_bytes=60 * 1024 * 1024
        ),
        cost_estimate=pl.CostEstimate(
            flops=9_000_000_000, bytes_accessed=6_000_000, transcendentals=8_400_000
        ),
    )(
        group_lens,
        dispatch,
        queries.reshape(NZ, 2, 16, 2 * HD),
        keys,
        values,
        out_weight,
    )


def solution(mesh):
    return jax.shard_map(
        body,
        mesh=mesh,
        in_specs=(P("ctx", "head"), P("ctx", "head"), P("ctx", "head"), P(), P(), P("head", None)),
        out_specs=P(("ctx", "head"), None),
        check_vma=False,
    )
```

time: 75.5 us -> 70.4 us (0.932)
  Pallas kernels: 73.6 us -> 68.6 us
    pallas_call x1, Pallas kernels: 73.6 us -> 68.6 us  [body(): pl.pallas_call(kernel, out_shape=jax.ShapeDtypeStruct((ROWS // NZ, D), bf...]
where the time goes in v3:
time: 70.4 us; the launch traced here: 70.2 us
  Pallas kernels  68.6 us (97%)
  local copies, waits for them, and re-layouts  1.62 us (2%)
    pallas_call x1, Pallas kernels, body(): pl.pallas_call(kernel, out_shape=jax.ShapeDtypeStruct((ROWS // NZ, D), bf...  68.6 us
    unnamed x1, local copies, waits for them, and re-layouts  1.62 us

profile of v3, /device:TPU:1, one launch (start us, length us, event | category | flops | bytes accessed | tf_op | source)
XLA Modules:
  0.0 70.2 jit_solution(11113490967011570892)
XLA Ops:
  0.0 68.6 %shard_map.64 = bf16[32,3072]{1,0:T(8,128)(2,1)} custom-call(s32[32]{0:T(128)} %lens_in.1, s32[256]{0:T(256)} %disp_in.1, bf16[8,2,16,256]{3,2,1,0:T(8,128)(2,1)} %bitcast.1, bf16[256,256]{1,0:T(8,128)(2,1)} %k_in.1, bf16[256,256]{1,0:T(8,128)(2,1)} %v_in.1, bf16[256,3072]{1,0:T(8,128)(2,1)} %w_in.1), custom_call_target="tpu_custom_call" | custom-call | flops 8999999488 | bytes 6000000 | tf_op jit(solution)/shard_map/pallas_call | solution.py:372
  68.6 1.6 %copy.8 = bf16[32,3072]{1,0:T(8,128)(2,1)} copy(bf16[32,3072]{1,0:T(8,128)(2,1)} %shard_map.64) | data formatting | bytes 393216

commit v4 on v3

--- a/solution.py
+++ b/solution.py
@@ -163,7 +163,8 @@
         konehot[pl.ds(pl.multiple_of(s * SLICE, SLICE), SLICE), :] = inside.astype(jnp.bfloat16)
         return 0
 
-    lax.fori_loop(0, KEYS // SLICE, key_marks, 0)
+    def mark(b):
+        lax.fori_loop(8 * b, 8 * b + 8, key_marks, 0)
 
     def query_marks(i, _):
         owner, half, s = i // 8, lax.rem(i // 4, 2), lax.rem(i, 4)
@@ -183,6 +184,7 @@
     vt[HD:, :] = jnp.ones((16, KEYS), jnp.bfloat16)
 
     lax.fori_loop(0, NX * 8, query_marks, 0)
+    mark(0)
     for copy in swaps:
         copy.wait_recv()
     turn(0)
@@ -255,11 +257,15 @@
 
     buffers = ((score_a, peak_a), (score_b, peak_b))
 
-    def stage(d, units, tasks):
+    def stage(d, units, tasks, marks=(), ready=None):
         beside(scores(d, *units[0], *buffers[0]))
+        if ready is not None:
+            ready()
         for i, unit in enumerate(units):
             for task in tasks[i : i + 1]:
                 arrive(*task)
+            if i < len(marks):
+                mark(marks[i])
             streams = [weigh(d, *unit, *buffers[i % 2])]
             if i + 1 < len(units):
                 streams.insert(0, scores(d, *units[i + 1], *buffers[(i + 1) % 2]))
@@ -289,18 +295,26 @@
     stage(0, order[2:6], arrivals(1)[2:])
     for copy in q_far:
         copy.wait_recv()
-    stage(0, order[:2], [])
-    for d in range(1, 4):
-        if d == 3:
-            drain()
+    stage(0, order[:2], [], (1, 7))
+    for d in range(1, 3):
         turn(d)
         turn(NY - d)
-        stage(d, order, arrivals(d + 1))
-    turn(4)
-    stage(4, order, [])
-
-    swaps = []
-    for p in range(2):
+        stage(d, order, arrivals(d + 1), (d + 1, NY - d - 1))
+    turn(3)
+    turn(5)
+    stage(3, order, [], (4,))
+    drain()
+    for task in arrivals(4)[:2]:
+        arrive(*task)
+
+    def last_values():
+        for task in arrivals(4)[2:]:
+            arrive(*task)
+        turn(4)
+
+    stage(4, order[0::2][:3] + order[1::2][:3] + order[6:], [], ready=last_values)
+
+    def finish(p):
         slots = [3 * p + k for k in range(3)]
         for slot in slots:
             for copy in given[slot]:
@@ -315,10 +329,9 @@
             o = o + yo_recv[slot].astype(jnp.float32) * (f * inverse)
         o = jnp.transpose(o).astype(jnp.bfloat16)
         att_send[p] = jnp.where(c == 0, o[PIECE:], o[:PIECE])
-        swaps.append(send(att_send.at[p], att.at[p, c], at_s.at[p], at_r.at[p], sibling))
+        back = send(att_send.at[p], att.at[p, c], at_s.at[p], at_r.at[p], sibling)
         att[p, c] = jnp.where(c == 0, o[:PIECE], o[PIECE:])
-
-    load_w.wait()
+        back.wait_recv()
 
     def project(p):
         rows = jnp.concatenate([att[p, 0], att[p, 1]], axis=1)
@@ -333,28 +346,34 @@
 
     zhops = {}
     half = D // 2
-    for j in range(1, 5):
+
+    def z_step(j, p):
+        for short in range(2):
+            if short and j == 4:
+                continue
+            for h in range(2):
+                travel = (2 * p - 1) * (1 - 2 * short) * (1 - 2 * h)
+                owner = ring(z, travel * (5 - j - short), NZ)
+                r = proj[p, owner, :, h * half : (h + 1) * half]
+                slot = (2 * p + h) * 7 + 4 * short + j - 1
+                if j > 1:
+                    zhops[slot - 1].wait_recv()
+                    r = r + z_recv[slot - 1].astype(jnp.float32)
+                z_send[slot] = r.astype(jnp.bfloat16)
+                zhops[slot] = send(
+                    z_send.at[slot], z_recv.at[slot], z_s.at[slot], z_r.at[slot], z_dev(travel)
+                )
+
+    load_w.wait()
+    for p in range(2):
+        finish(p)
+        project(p)
+        z_step(1, p)
+    for j in range(2, 5):
         if j == 3:
             drain()
-        for short in range(2):
-            for p in range(2):
-                if short and j == 4:
-                    continue
-                if j == 1 and not short:
-                    swaps[p].wait_recv()
-                    project(p)
-                for h in range(2):
-                    travel = (2 * p - 1) * (1 - 2 * short) * (1 - 2 * h)
-                    owner = ring(z, travel * (5 - j - short), NZ)
-                    r = proj[p, owner, :, h * half : (h + 1) * half]
-                    slot = (2 * p + h) * 7 + 4 * short + j - 1
-                    if j > 1:
-                        zhops[slot - 1].wait_recv()
-                        r = r + z_recv[slot - 1].astype(jnp.float32)
-                    z_send[slot] = r.astype(jnp.bfloat16)
-                    zhops[slot] = send(
-                        z_send.at[slot], z_recv.at[slot], z_s.at[slot], z_r.at[slot], z_dev(travel)
-                    )
+        for p in range(2):
+            z_step(j, p)
     for p in range(2):
         for h in range(2):
             r = proj[p, z, :, h * half : (h + 1) * half]

time: 70.4 us -> 67.7 us (0.962); the launches traced: 70.2 us -> 66.5 us
  Pallas kernels: 68.6 us -> 64.9 us
    pallas_call x1, Pallas kernels: 68.6 us -> 64.9 us  [body(): pl.pallas_call(kernel, out_shape=jax.ShapeDtypeStruct((ROWS // NZ, D), bf...]
where the time goes in v4:
time: 67.7 us; the launch traced here: 66.5 us
  Pallas kernels  64.9 us (96%)
  local copies, waits for them, and re-layouts  1.62 us (2%)
    pallas_call x1, Pallas kernels, body(): pl.pallas_call(kernel, out_shape=jax.ShapeDtypeStruct((ROWS // NZ, D), bf...  64.9 us
    unnamed x1, local copies, waits for them, and re-layouts  1.62 us

profile of v4, /device:TPU:1, one launch (start us, length us, event | category | flops | bytes accessed | tf_op | source)
XLA Modules:
  0.0 66.5 jit_solution(16120314584146576728)
XLA Ops:
  0.0 64.9 %shard_map.64 = bf16[32,3072]{1,0:T(8,128)(2,1)} custom-call(s32[32]{0:T(128)} %lens_in.1, s32[256]{0:T(256)} %disp_in.1, bf16[8,2,16,256]{3,2,1,0:T(8,128)(2,1)} %bitcast.1, bf16[256,256]{1,0:T(8,128)(2,1)} %k_in.1, bf16[256,256]{1,0:T(8,128)(2,1)} %v_in.1, bf16[256,3072]{1,0:T(8,128)(2,1)} %w_in.1), custom_call_target="tpu_custom_call" | custom-call | flops 8999999488 | bytes 6000000 | tf_op jit(solution)/shard_map/pallas_call | solution.py:391
  64.9 1.6 %copy.8 = bf16[32,3072]{1,0:T(8,128)(2,1)} copy(bf16[32,3072]{1,0:T(8,128)(2,1)} %shard_map.64) | data formatting | bytes 393216

commit v5 on v4

--- a/solution.py
+++ b/solution.py
@@ -333,54 +333,51 @@
         att[p, c] = jnp.where(c == 0, o[:PIECE], o[PIECE:])
         back.wait_recv()
 
-    def project(p):
+    part = D // 4
+
+    def project(p, h):
         rows = jnp.concatenate([att[p, 0], att[p, 1]], axis=1)
 
-        def columns(n, _):
-            cut = pl.ds(pl.multiple_of(n * 768, 768), 768)
-            r = jnp.dot(rows, wbuf[:, cut], preferred_element_type=jnp.float32)
-            proj[p, :, :, cut] = r.reshape(NZ, 16, 768)
-            return 0
-
-        lax.fori_loop(0, D // 768, columns, 0)
+        cut = slice(h * part, (h + 1) * part)
+        r = jnp.dot(rows, wbuf[:, cut], preferred_element_type=jnp.float32)
+        proj[p, :, :, cut] = r.reshape(NZ, 16, part)
 
     zhops = {}
-    half = D // 2
-
-    def z_step(j, p):
-        for short in range(2):
-            if short and j == 4:
-                continue
-            for h in range(2):
-                travel = (2 * p - 1) * (1 - 2 * short) * (1 - 2 * h)
-                owner = ring(z, travel * (5 - j - short), NZ)
-                r = proj[p, owner, :, h * half : (h + 1) * half]
-                slot = (2 * p + h) * 7 + 4 * short + j - 1
-                if j > 1:
-                    zhops[slot - 1].wait_recv()
-                    r = r + z_recv[slot - 1].astype(jnp.float32)
-                z_send[slot] = r.astype(jnp.bfloat16)
-                zhops[slot] = send(
-                    z_send.at[slot], z_recv.at[slot], z_s.at[slot], z_r.at[slot], z_dev(travel)
-                )
+
+    def z_hop(j, p, short, h):
+        travel = (2 * p - 1) * (1 - 2 * short) * (1 - 2 * (h % 2))
+        owner = ring(z, travel * (5 - j - short), NZ)
+        r = proj[p, owner, :, h * part : (h + 1) * part]
+        slot = (4 * p + h) * 7 + 4 * short + j - 1
+        if j > 1:
+            zhops[slot - 1].wait_recv()
+            r = r + z_recv[slot - 1].astype(jnp.float32)
+        z_send[slot] = r.astype(jnp.bfloat16)
+        zhops[slot] = send(
+            z_send.at[slot], z_recv.at[slot], z_s.at[slot], z_r.at[slot], z_dev(travel)
+        )
 
     load_w.wait()
     for p in range(2):
         finish(p)
-        project(p)
-        z_step(1, p)
+        for h in range(4):
+            project(p, h)
+            for short in range(2):
+                z_hop(1, p, short, h)
     for j in range(2, 5):
         if j == 3:
             drain()
         for p in range(2):
-            z_step(j, p)
+            for short in range(2 if j < 4 else 1):
+                for h in range(4):
+                    z_hop(j, p, short, h)
     for p in range(2):
-        for h in range(2):
-            r = proj[p, z, :, h * half : (h + 1) * half]
-            for slot in ((2 * p + h) * 7 + 6, (2 * p + h) * 7 + 3):
+        for h in range(4):
+            r = proj[p, z, :, h * part : (h + 1) * part]
+            for slot in ((4 * p + h) * 7 + 6, (4 * p + h) * 7 + 3):
                 zhops[slot].wait_recv()
                 r = r + z_recv[slot].astype(jnp.float32)
-            out[p * 16 : (p + 1) * 16, h * half : (h + 1) * half] = r.astype(jnp.bfloat16)
+            out[p * 16 : (p + 1) * 16, h * part : (h + 1) * part] = r.astype(jnp.bfloat16)
     drain()
 
 
@@ -417,11 +414,11 @@
             pltpu.VMEM((2, PIECE, HD), bf),
             pltpu.VMEM((2 * HD, D), bf),
             pltpu.VMEM((2, NZ, 16, D), f32),
-            pltpu.VMEM((28, 16, D // 2), bf),
-            pltpu.VMEM((28, 16, D // 2), bf),
+            pltpu.VMEM((56, 16, D // 4), bf),
+            pltpu.VMEM((56, 16, D // 4), bf),
             dma((7,)), dma((4,)), dma((4,)), dma((12,)), dma((12,)), dma((28,)), dma((28,)),
             dma((6,)), dma((6,)), dma((6,)), dma((6,)), dma((2,)), dma((2,)),
-            dma((28,)), dma((28,)),
+            dma((56,)), dma((56,)),
         ],
         compiler_params=pltpu.CompilerParams(
             collective_id=0, has_side_effects=True, vmem_limit_bytes=60 * 1024 * 1024

time: 67.7 us -> 67.7 us (level)
  the two profiles are of different devices: /device:TPU:1 before, /device:TPU:24 now
where the time goes in v5:
time: 67.7 us; the launch traced here: 67.5 us
  Pallas kernels  65.9 us (97%)
  local copies, waits for them, and re-layouts  1.62 us (2%)
    pallas_call x1, Pallas kernels, body(): pl.pallas_call(kernel, out_shape=jax.ShapeDtypeStruct((ROWS // NZ, D), bf...  65.9 us
    unnamed x1, local copies, waits for them, and re-layouts  1.62 us

profile of v5, /device:TPU:24, one launch (start us, length us, event | category | flops | bytes accessed | tf_op | source)
XLA Modules:
  0.0 67.5 jit_solution(10676509895101501376)
XLA Ops:
  0.0 65.9 %shard_map.64 = bf16[32,3072]{1,0:T(8,128)(2,1)} custom-call(s32[32]{0:T(128)} %lens_in.1, s32[256]{0:T(256)} %disp_in.1, bf16[8,2,16,256]{3,2,1,0:T(8,128)(2,1)} %bitcast.1, bf16[256,256]{1,0:T(8,128)(2,1)} %k_in.1, bf16[256,256]{1,0:T(8,128)(2,1)} %v_in.1, bf16[256,3072]{1,0:T(8,128)(2,1)} %w_in.1), custom_call_target="tpu_custom_call" | custom-call | flops 8999999488 | bytes 6000000 | tf_op jit(solution)/shard_map/pallas_call | solution.py:388
  65.9 1.6 %copy.8 = bf16[32,3072]{1,0:T(8,128)(2,1)} copy(bf16[32,3072]{1,0:T(8,128)(2,1)} %shard_map.64) | data formatting | bytes 393216
